TPU v7x, 32 devices: a whole 2x2x4 slice. The times are simulated.
32 devices in a mesh: dp: 8 (over z, y), tensor: 4 (over x, core).
Axes of the slice: x: 2, y: 2, z: 4, core: 2. Of those that a mesh axis runs over, the one named last changes fastest.
Arguments:
- tokens: bfloat16 [16384, 768], P('dp'), may hold values from -6 to 6
- cotangent: bfloat16 [16384, 768], P('dp'), may hold values from -6 to 6
- row_lengths: int32 [32], P('dp'), may hold values from 64 to 512
- present: int32 [32, 64], P('dp'), may hold values 0 or 1
- groups: int32 [32, 512], P('dp'), may hold values from 0 to 63, never falling along the last dimension, each value on 1 to 16 neighbouring positions
- attn_weight: float32 [3, 768, 768], P(None, 'dp', 'tensor'), may hold values from -0.21875 to 0.21875
- attn_first: float32 [3, 768, 768], P(None, 'dp', 'tensor'), may hold values from -24 to 24
- attn_second: float32 [3, 768, 768], P(None, 'dp', 'tensor'), may hold values from 64 to 256
- mix_weight: float32 [768, 768], P('tensor', 'dp'), may hold values from -2.5 to 2.5
- mix_first: float32 [768, 768], P('tensor', 'dp'), may hold values from -32 to 32
- mix_second: float32 [768, 768], P('tensor', 'dp'), may hold values from 128 to 512
- up_weight: float32 [768, 3072], P('dp', 'tensor'), may hold values from -0.21875 to 0.21875
- up_first: float32 [768, 3072], P('dp', 'tensor'), may hold values from -96 to 96
- up_second: float32 [768, 3072], P('dp', 'tensor'), may hold values from 1024 to 4096
- down_weight: float32 [3072, 768], P('tensor', 'dp'), may hold values from -0.109375 to 0.109375
- down_first: float32 [3072, 768], P('tensor', 'dp'), may hold values from -192 to 192
- down_second: float32 [3072, 768], P('tensor', 'dp'), may hold values from 4096 to 16384
- head_bias: float32 [2, 768], P(None, ('tensor', 'dp')), may hold values from -4 to 4
- head_first: float32 [2, 768], P(None, ('tensor', 'dp')), may hold values from -512 to 512
- head_second: float32 [2, 768], P(None, ('tensor', 'dp')), may hold values from 8192 to 32768
- wide_bias: float32 [3072], P(('tensor', 'dp')), may hold values from -4 to 4
- wide_first: float32 [3072], P(('tensor', 'dp')), may hold values from -512 to 512
- wide_second: float32 [3072], P(('tensor', 'dp')), may hold values from 8192 to 32768
- norm_gains: float32 [2, 768], P(None, 'dp'), may hold values from 0.5 to 1.5
- gain_first: float32 [2, 768], P(None, 'dp'), may hold values from -512 to 512
- gain_second: float32 [2, 768], P(None, 'dp'), may hold values from 8192 to 32768
- shift_bias: float32 [4, 768], P(None, 'dp'), may hold values from -4 to 4
- shift_first: float32 [4, 768], P(None, 'dp'), may hold values from -512 to 512
- shift_second: float32 [4, 768], P(None, 'dp'), may hold values from 8192 to 32768
Outputs:
- layer_out: bfloat16 [16384, 768], P('dp')
- tokens_grad: bfloat16 [16384, 768], P('dp')
- attn_weight_new: float32 [3, 768, 768], P(None, 'dp', 'tensor')
- attn_first_new: float32 [3, 768, 768], P(None, 'dp', 'tensor')
- attn_second_new: float32 [3, 768, 768], P(None, 'dp', 'tensor')
- mix_weight_new: float32 [768, 768], P('tensor', 'dp')
- mix_first_new: float32 [768, 768], P('tensor', 'dp')
- mix_second_new: float32 [768, 768], P('tensor', 'dp')
- up_weight_new: float32 [768, 3072], P('dp', 'tensor')
- up_first_new: float32 [768, 3072], P('dp', 'tensor')
- up_second_new: float32 [768, 3072], P('dp', 'tensor')
- down_weight_new: float32 [3072, 768], P('tensor', 'dp')
- down_first_new: float32 [3072, 768], P('tensor', 'dp')
- down_second_new: float32 [3072, 768], P('tensor', 'dp')
- head_bias_new: float32 [2, 768], P(None, ('tensor', 'dp'))
- head_first_new: float32 [2, 768], P(None, ('tensor', 'dp'))
- head_second_new: float32 [2, 768], P(None, ('tensor', 'dp'))
- wide_bias_new: float32 [3072], P(('tensor', 'dp'))
- wide_first_new: float32 [3072], P(('tensor', 'dp'))
- wide_second_new: float32 [3072], P(('tensor', 'dp'))
- norm_gains_new: float32 [2, 768], P(None, 'dp')
- gain_first_new: float32 [2, 768], P(None, 'dp')
- gain_second_new: float32 [2, 768], P(None, 'dp')
- shift_bias_new: float32 [4, 768], P(None, 'dp')
- shift_first_new: float32 [4, 768], P(None, 'dp')
- shift_second_new: float32 [4, 768], P(None, 'dp')
- norm_pairs: float32 [2, 15], replicated
Inputs may be any that keep to these rules, and one draw needn't show every extreme that they name: Along a row the group ids never fall; every one of the 64 groups holds 1 to 16 slots.
All inputs are finite; a program needn't handle non-finite values. No bound on the sum of `present` on one device may be relied on, other than what follows from the above.
Results may differ from a plain program's by a relative error of at most 0.023.
Values may be sent and summed in bfloat16 or wider, within the bound.
No kernel may reach another device: no remote copies, remote signals or barrier semaphores. Data moves between devices by JAX's collectives and lax.ppermute only.
A program may use at most 128 MiB of HBM per device.

v0:
```python
from functools import partial

import jax
import jax.numpy as jnp
from jax import lax
from jax.sharding import PartitionSpec as P

HEAD = 64


def layer_norm(summed):
    center = summed - jnp.mean(summed, axis=-1, keepdims=True)
    spread = jnp.mean(center * center, axis=-1, keepdims=True)
    scaled = lax.rsqrt(spread + 1e-05)
    return (center * scaled, scaled)


def norm_back(upstream, normal, scaled):
    inner_sum = (
        upstream
        - jnp.mean(upstream, axis=-1, keepdims=True)
        - normal * jnp.mean(upstream * normal, axis=-1, keepdims=True)
    )
    return scaled * inner_sum


def visibility(length, present_row, group_row):
    positions = jnp.arange(group_row.shape[0])
    feature_ids = jnp.arange(present_row.shape[0])
    present_key = jnp.sum(
        (group_row[:, None] == feature_ids[None, :]) * present_row[None, :], axis=1
    )
    key_open = (positions < length) & (present_key == 1)
    return key_open[None, :] | (group_row[:, None] == group_row[None, :])


def row_scores(queries, key_rows, visible):
    scale = queries.shape[-1] ** (-0.5)
    scores = (
        jnp.einsum("qhd,khd->hqk", queries, key_rows, preferred_element_type=jnp.float32) * scale
    )
    return jnp.where(visible[None], scores, -1e30)


def row_forward(row_item):
    queries, key_rows, value_rows, visible = row_item
    scores = row_scores(queries, key_rows, visible)
    largest = jnp.max(scores, axis=-1, keepdims=True)
    exponent = jnp.exp(scores - largest)
    row_total = jnp.sum(exponent, axis=-1, keepdims=True)
    probs_low = (exponent / row_total).astype(jnp.bfloat16)
    context = jnp.einsum("hqk,khd->qhd", probs_low, value_rows, preferred_element_type=jnp.float32)
    return (context.astype(jnp.bfloat16), largest + jnp.log(row_total))


def row_backward(row_item):
    queries, key_rows, value_rows, visible, log_total, context_grad = row_item
    scale = queries.shape[-1] ** (-0.5)
    scores = row_scores(queries, key_rows, visible)
    softmax_probs = jnp.exp(scores - log_total)
    probs_low = softmax_probs.astype(jnp.bfloat16)
    value_grad = jnp.einsum(
        "hqk,qhd->khd", probs_low, context_grad, preferred_element_type=jnp.float32
    )
    probs_grad = jnp.einsum(
        "qhd,khd->hqk", context_grad, value_rows, preferred_element_type=jnp.float32
    )
    inner_sum = jnp.sum(softmax_probs * probs_grad, axis=-1, keepdims=True)
    scores_grad = (softmax_probs * (probs_grad - inner_sum)).astype(jnp.bfloat16)
    query_grad = (
        jnp.einsum("hqk,khd->qhd", scores_grad, key_rows, preferred_element_type=jnp.float32)
        * scale
    )
    key_grad = (
        jnp.einsum("hqk,qhd->khd", scores_grad, queries, preferred_element_type=jnp.float32) * scale
    )
    return (
        query_grad.astype(jnp.bfloat16),
        key_grad.astype(jnp.bfloat16),
        value_grad.astype(jnp.bfloat16),
    )


def square_sums(array, piece_count, weight_factor):
    if piece_count == 1:
        return [jnp.sum(array * array) * weight_factor]
    return [jnp.sum(array[member] * array[member]) * weight_factor for member in range(piece_count)]


def trust_factor(trust, offset, piece_count, rank_count):
    if piece_count == 1:
        return trust[offset]
    return trust[offset : offset + piece_count].reshape((piece_count,) + (1,) * (rank_count - 1))


def on_device(
    tokens,
    cotangent,
    row_lengths,
    present,
    groups,
    attn_weight,
    attn_first,
    attn_second,
    mix_weight,
    mix_first,
    mix_second,
    up_weight,
    up_first,
    up_second,
    down_weight,
    down_first,
    down_second,
    head_bias,
    head_first,
    head_second,
    wide_bias,
    wide_first,
    wide_second,
    norm_gains,
    gain_first,
    gain_second,
    shift_bias,
    shift_first,
    shift_second,
):
    bfloat = jnp.bfloat16
    single = jnp.float32
    attn_low, mix_low, up_low, down_low, head_low, wide_low, gain_low, shift_low = (
        lax.all_gather(attn_weight.astype(bfloat), "dp", axis=1, tiled=True),
        lax.all_gather(mix_weight.astype(bfloat), "dp", axis=1, tiled=True),
        lax.all_gather(up_weight.astype(bfloat), "dp", axis=0, tiled=True),
        lax.all_gather(down_weight.astype(bfloat), "dp", axis=1, tiled=True),
        lax.all_gather(head_bias.astype(bfloat), "dp", axis=1, tiled=True),
        lax.all_gather(wide_bias.astype(bfloat), "dp", axis=0, tiled=True),
        lax.all_gather(norm_gains.astype(bfloat), "dp", axis=1, tiled=True),
        lax.all_gather(shift_bias.astype(bfloat), "dp", axis=1, tiled=True),
    )
    gain_float = gain_low.astype(single)
    shift_float = shift_low.astype(single)
    row_count = row_lengths.shape[0]
    row_slots = groups.shape[1]
    local_width = attn_low.shape[2]
    row_shape = (row_count, row_slots, local_width // HEAD, HEAD)
    projected = jnp.einsum("td,kdc->ktc", tokens, attn_low, preferred_element_type=single)
    queries = (projected[0] + head_low[0].astype(single)).astype(bfloat).reshape(row_shape)
    key_rows = projected[1].astype(bfloat).reshape(row_shape)
    value_rows = (projected[2] + head_low[1].astype(single)).astype(bfloat).reshape(row_shape)
    visible = jax.vmap(visibility)(row_lengths, present, groups)
    context, log_total = lax.map(row_forward, (queries, key_rows, value_rows, visible))
    context = context.reshape(row_count * row_slots, local_width)
    attn_part = jnp.dot(context, mix_low, preferred_element_type=single)
    attended = (
        lax.psum(attn_part.astype(jnp.bfloat16), "tensor").astype(jnp.float32) + shift_float[0]
    )
    normal_one, scaled_one = layer_norm(tokens.astype(single) + attended)
    normed = normal_one * gain_float[0] + shift_float[1]
    normed_low = normed.astype(bfloat)
    hidden = jnp.dot(normed_low, up_low, preferred_element_type=single) + wide_low.astype(single)
    active, gelu_back = jax.vjp(partial(jax.nn.gelu, approximate=False), hidden)
    active_low = active.astype(bfloat)
    ffn_part = jnp.dot(active_low, down_low, preferred_element_type=single)
    summed_two = (
        normed
        + lax.psum(ffn_part.astype(jnp.bfloat16), "tensor").astype(jnp.float32)
        + shift_float[2]
    )
    normal_two, scaled_two = layer_norm(summed_two)
    layer_out = (normal_two * gain_float[1] + shift_float[3]).astype(bfloat)
    upstream = cotangent.astype(single)
    gain_two_grad = jnp.sum(upstream * normal_two, axis=0)
    shift_three_grad = jnp.sum(upstream, axis=0)
    back_two = norm_back(upstream * gain_float[1], normal_two, scaled_two)
    shift_two_grad = jnp.sum(back_two, axis=0)
    back_two_low = back_two.astype(bfloat)
    down_grad = jnp.einsum("tf,td->fd", active_low, back_two_low, preferred_element_type=single)
    active_grad = jnp.einsum("td,fd->tf", back_two_low, down_low, preferred_element_type=single)
    hidden_grad = gelu_back(active_grad)[0].astype(bfloat)
    wide_grad = jnp.sum(hidden_grad.astype(single), axis=0)
    up_grad = jnp.einsum("td,tf->df", normed_low, hidden_grad, preferred_element_type=single)
    normed_part = jnp.einsum("tf,df->td", hidden_grad, up_low, preferred_element_type=single)
    normed_grad = back_two + lax.psum(normed_part.astype(jnp.bfloat16), "tensor").astype(
        jnp.float32
    )
    gain_one_grad = jnp.sum(normed_grad * normal_one, axis=0)
    shift_one_grad = jnp.sum(normed_grad, axis=0)
    back_one = norm_back(normed_grad * gain_float[0], normal_one, scaled_one)
    shift_zero_grad = jnp.sum(back_one, axis=0)
    back_one_low = back_one.astype(bfloat)
    mix_grad = jnp.einsum("tc,td->cd", context, back_one_low, preferred_element_type=single)
    context_grad = jnp.einsum(
        "td,cd->tc", back_one_low, mix_low, preferred_element_type=single
    ).astype(bfloat)
    query_grad, key_grad, value_grad = lax.map(
        row_backward,
        (queries, key_rows, value_rows, visible, log_total, context_grad.reshape(row_shape)),
    )
    token_count = row_count * row_slots
    stacked = jnp.stack(
        [
            query_grad.reshape(token_count, local_width),
            key_grad.reshape(token_count, local_width),
            value_grad.reshape(token_count, local_width),
        ]
    )
    head_grad = jnp.stack(
        [jnp.sum(stacked[0].astype(single), axis=0), jnp.sum(stacked[2].astype(single), axis=0)]
    )
    attn_grad = jnp.einsum("td,ktc->kdc", tokens, stacked, preferred_element_type=single)
    token_part = jnp.einsum("ktc,kdc->td", stacked, attn_low, preferred_element_type=single)
    tokens_grad = (
        back_one + lax.psum(token_part.astype(jnp.bfloat16), "tensor").astype(jnp.float32)
    ).astype(bfloat)
    gain_grad = jnp.stack([gain_one_grad, gain_two_grad])
    shift_grad = jnp.stack([shift_zero_grad, shift_one_grad, shift_two_grad, shift_three_grad])
    attn_sum_grad, mix_sum, up_sum, down_sum, head_sum, wide_sum, gain_sum, shift_sum = (
        lax.psum_scatter(attn_grad, "dp", scatter_dimension=1, tiled=True),
        lax.psum_scatter(mix_grad, "dp", scatter_dimension=1, tiled=True),
        lax.psum_scatter(up_grad, "dp", scatter_dimension=0, tiled=True),
        lax.psum_scatter(down_grad, "dp", scatter_dimension=1, tiled=True),
        lax.psum_scatter(head_grad, "dp", scatter_dimension=1, tiled=True),
        lax.psum_scatter(wide_grad, "dp", scatter_dimension=0, tiled=True),
        lax.psum_scatter(gain_grad, "dp", scatter_dimension=1, tiled=True),
        lax.psum_scatter(shift_grad, "dp", scatter_dimension=1, tiled=True),
    )
    masters = (
        attn_weight,
        mix_weight,
        up_weight,
        down_weight,
        head_bias,
        wide_bias,
        norm_gains,
        shift_bias,
    )
    firsts = (
        attn_first,
        mix_first,
        up_first,
        down_first,
        head_first,
        wide_first,
        gain_first,
        shift_first,
    )
    seconds = (
        attn_second,
        mix_second,
        up_second,
        down_second,
        head_second,
        wide_second,
        gain_second,
        shift_second,
    )
    reduced = (attn_sum_grad, mix_sum, up_sum, down_sum, head_sum, wide_sum, gain_sum, shift_sum)
    piece_counts = (3, 1, 1, 1, 2, 1, 2, 4)
    share = 1.0 / lax.axis_size("tensor")
    weight_factors = (1.0, 1.0, 1.0, 1.0, 1.0, 1.0, share, share)
    new_firsts, new_seconds, updates, weight_sq, update_sq = ([], [], [], [], [])
    for master, first_old, second_old, gradient, piece_count, weight_factor in zip(
        masters, firsts, seconds, reduced, piece_counts, weight_factors
    ):
        first_new = 0.5 * first_old + 0.5 * gradient
        second_new = 0.5 * second_old + 0.5 * gradient * gradient
        update = first_new / (jnp.sqrt(second_new) + 1e-06) + 0.01 * master
        new_firsts.append(first_new)
        new_seconds.append(second_new)
        updates.append(update)
        weight_sq.extend(square_sums(master, piece_count, weight_factor))
        update_sq.extend(square_sums(update, piece_count, weight_factor))
    square_totals = lax.psum(
        jnp.stack([jnp.stack(weight_sq), jnp.stack(update_sq)]), ("dp", "tensor")
    )
    norm_pairs = jnp.sqrt(square_totals)
    trust = norm_pairs[0] / (norm_pairs[1] + 1e-06)
    new_masters = []
    offset = 0
    for master, update, piece_count in zip(masters, updates, piece_counts):
        factor = trust_factor(trust, offset, piece_count, master.ndim)
        new_masters.append(master - 0.5 * factor * update)
        offset = offset + piece_count
    return (
        layer_out,
        tokens_grad,
        new_masters[0],
        new_firsts[0],
        new_seconds[0],
        new_masters[1],
        new_firsts[1],
        new_seconds[1],
        new_masters[2],
        new_firsts[2],
        new_seconds[2],
        new_masters[3],
        new_firsts[3],
        new_seconds[3],
        new_masters[4],
        new_firsts[4],
        new_seconds[4],
        new_masters[5],
        new_firsts[5],
        new_seconds[5],
        new_masters[6],
        new_firsts[6],
        new_seconds[6],
        new_masters[7],
        new_firsts[7],
        new_seconds[7],
        norm_pairs,
    )


def solution(mesh):
    return jax.shard_map(
        on_device,
        mesh=mesh,
        in_specs=(
            P("dp", None),
            P("dp", None),
            P("dp"),
            P("dp", None),
            P("dp", None),
            P(None, "dp", "tensor"),
            P(None, "dp", "tensor"),
            P(None, "dp", "tensor"),
            P("tensor", "dp"),
            P("tensor", "dp"),
            P("tensor", "dp"),
            P("dp", "tensor"),
            P("dp", "tensor"),
            P("dp", "tensor"),
            P("tensor", "dp"),
            P("tensor", "dp"),
            P("tensor", "dp"),
            P(None, ("tensor", "dp")),
            P(None, ("tensor", "dp")),
            P(None, ("tensor", "dp")),
            P(("tensor", "dp")),
            P(("tensor", "dp")),
            P(("tensor", "dp")),
            P(None, "dp"),
            P(None, "dp"),
            P(None, "dp"),
            P(None, "dp"),
            P(None, "dp"),
            P(None, "dp"),
        ),
        out_specs=(
            P("dp", None),
            P("dp", None),
            P(None, "dp", "tensor"),
            P(None, "dp", "tensor"),
            P(None, "dp", "tensor"),
            P("tensor", "dp"),
            P("tensor", "dp"),
            P("tensor", "dp"),
            P("dp", "tensor"),
            P("dp", "tensor"),
            P("dp", "tensor"),
            P("tensor", "dp"),
            P("tensor", "dp"),
            P("tensor", "dp"),
            P(None, ("tensor", "dp")),
            P(None, ("tensor", "dp")),
            P(None, ("tensor", "dp")),
            P(("tensor", "dp")),
            P(("tensor", "dp")),
            P(("tensor", "dp")),
            P(None, "dp"),
            P(None, "dp"),
            P(None, "dp"),
            P(None, "dp"),
            P(None, "dp"),
            P(None, "dp"),
            P(),
        ),
        check_vma=False,
    )
```

profile of v0, /device:TPU:0, one launch (start us, length us, event | category | flops | bytes accessed | tf_op | source)
XLA Modules:
  0.0 908.8 jit_solution(8584713637614694734)
XLA Ops:
  9.2 38.6 %all_gather.24 = bf16[3,768,192]{2,0,1:T(4,128)(2,1)S(1)} all-gather(bf16[3,96,192]{2,0,1:T(4,128)(2,1)S(1)} %copy.160), channel_id=1, replica_groups=mesh['dp'=8,'tensor'=4] {'dp'}, dimensions={1}, use_global_device_ids=true | all-gather | bytes 995328 | tf_op jit(solution)/shard_map/all_gather | solution.py:130
  58.8 19.2 %all-gather = bf16[8,24,2]{1,2,0:T(2,128)(2,1)S(1)} all-gather(bf16[1,24,2]{1,2,0:T(2,128)(2,1)S(1)} %convert_bitcast_fusion.2), channel_id=1, replica_groups=mesh['dp'=8,'tensor'=4] {'dp'}, dimensions={0}, use_global_device_ids=true | all-gather | bytes 864 | tf_op jit(solution)/shard_map/all_gather | solution.py:134
  85.8 15.5 %while.26 = (s32[]{:T(128)}, bf16[4,512,3,64]{1,3,2,0:T(8,128)(2,1)}, f32[4,3,512,1]{2,1,3,0:T(4,128)}, bf16[4,512,3,64]{1,3,2,0:T(8,128)(2,1)S(1)}, pred[4,512,...) while((s32[]{:T(128)}, ...), condition=%wide.region_4.5_spmd, body=%wide.region_1.4_spmd.sunk | while | flops 210860544 | bytes 11592281 | solution.py:150
  108.7 31.2 %all_gather.26 = bf16[192,768]{0,1:T(8,128)(2,1)S(1)} all-gather(bf16[192,96]{0,1:T(8,128)(2,1)} %copy.167), channel_id=1, replica_groups=mesh['dp'=8,'tensor'=4] {'dp'}, dimensions={1}, use_global_device_ids=true | all-gather | bytes 331776 | tf_op jit(solution)/shard_map/all_gather | solution.py:131
  147.4 16.5 %all-gather.1 = bf16[8,96,4]{1,2,0:T(4,128)(2,1)S(1)} all-gather(bf16[1,96,4]{1,2,0:T(4,128)(2,1)S(1)} %convert_bitcast_fusion), channel_id=1, replica_groups=mesh['dp'=8,'tensor'=4] {'dp'}, dimensions={0}, use_global_device_ids=true | all-gather | bytes 6912 | tf_op jit(solution)/shard_map/all_gather | solution.py:137
  166.7 18.0 %all-gather.2 = bf16[8,96,2]{1,2,0:T(2,128)(2,1)S(1)} all-gather(bf16[1,96,2]{1,2,0:T(2,128)(2,1)S(1)} %convert_bitcast_fusion.1), channel_id=1, replica_groups=mesh['dp'=8,'tensor'=4] {'dp'}, dimensions={0}, use_global_device_ids=true | all-gather | bytes 3456 | tf_op jit(solution)/shard_map/all_gather | solution.py:136
  190.3 17.7 %all-reduce = bf16[768]{0:T(1024)(128)(2,1)S(1)} all-reduce(bf16[768]{0:T(1024)(128)(2,1)S(1)} %dynamic-update-slice), channel_id=1, replica_groups=mesh['dp'=8,'tensor'=4] {'dp'}, use_global_device_ids=true, to_apply=%add | all-reduce | flops 768 | bytes 3072
  215.2 20.6 %multiply_convert_fusion.1 = (bf16[2048,768]{1,0:T(8,128)(2,1)}, f32[2048,768]{1,0:T(8,128)}, f32[2048,768]{1,0:T(8,128)}) fusion(f32[768]{0:T(1024)} %convert_element_type.165, bf16[768,768]{1,0:T(8,128)(2,1)} %all-gather.6.cloned.1.call-done, f32[768]{0:T(1024)} %get-tuple-element.367, f32[768]{0:T(1024)S(1)} %get-tuple-element.370, ...), kind=kOutput, calls=%fused_computation.83 | convolution fusion | flops 2533883904 | bytes 23228416 | tf_op jit(solution)/shard_map/dot_general | solution.py:159
  235.8 6.5 convolution_convert_fusion.1
  242.6 68.4 %all-reduce.11.cloned.1.call-done = bf16[2048,768]{1,0:T(8,128)(2,1)} async-done(((bf16[2048,768]{1,0:T(8,128)(2,1)}), bf16[2048,768]{1,0:T(8,128)(2,1)}) %all-reduce.11.cloned.1.call-update) | async-done | bytes 3145744 | tf_op jit(solution)/shard_map/psum | solution.py:165
  325.2 9.4 %convert_reduce_fusion.1 = (f32[768]{0:T(1024)}, bf16[2048,768]{1,0:T(8,128)(2,1)S(1)}) fusion(f32[2048,768]{1,0:T(8,128)S(1)} %bitcast.250, bf16[768,768]{0,1:T(8,128)(2,1)S(1)} %copy-done.57, f32[2048,768]{1,0:T(8,128)S(1)} %get-tuple-element.457, f32[2048,768]{1,0:T(8,128)} %get-tuple-element.471, f32[768]{0:T(1024)S(1)} %copy-done.43), kind=kOutput, calls=%fused_computation.74 | convolution fusion | flops 2444229888 | bytes 23205888 | tf_op jit(solution)/shard_map/td,fd->tf/dot_general | solution.py:177
  342.9 66.1 %all-reduce.13.cloned.1.call-done = bf16[2048,768]{1,0:T(8,128)(2,1)} async-done(((bf16[2048,768]{1,0:T(8,128)(2,1)}), bf16[2048,768]{1,0:T(8,128)(2,1)}) %all-reduce.13.cloned.1.call-update) | async-done | bytes 3145744 | tf_op jit(solution)/shard_map/psum | solution.py:182
  409.0 7.3 multiply_reduce_fusion.1
  416.4 8.1 fusion.111
  437.4 7.7 fusion.91
  445.1 7.9 fusion.77
  466.2 51.0 %while.27 = (s32[]{:T(128)}, bf16[4,512,3,64]{1,3,2,0:T(8,128)(2,1)}, bf16[4,512,3,64]{1,3,2,0:T(8,128)(2,1)}, bf16[4,512,3,64]{1,3,2,0:T(8,128)(2,1)}, bf16[4,5...) while((s32[]{:T(128)}, ...), condition=%wide.region_18.19_spmd, body=%wide.region_16.18_spmd.sunk | while | flops 510884352 | bytes 26381428 | solution.py:194
  560.8 21.7 %all-reduce.3 = (f32[2,192]{1,0:T(2,128)S(1)}, f32[768]{0:T(1024)S(1)}) all-reduce(f32[2,192]{1,0:T(2,128)S(1)} %pad_maximum_fusion.2, f32[768]{0:T(1024)S(1)} %copy-done.42), channel_id=6, replica_groups=mesh['dp'=8,'tensor'=4] {'dp'}, use_global_device_ids=true, to_apply=%region_47.48.clone | all-reduce | flops 1152 | bytes 9216
  583.9 6.7 bitcast_convert_fusion
  600.1 19.1 %reduce-scatter.22.cloned.1.call-done = f32[96,192]{1,0:T(8,128)} async-done(((f32[768,192]{1,0:T(8,128)}), f32[96,192]{1,0:T(8,128)}) %reduce-scatter.22.cloned.1.call-update) | async-done | bytes 73744
  621.5 69.8 %reduce-scatter.16.cloned.1.call-done = f32[96,768]{1,0:T(8,128)} async-done(((f32[768,768]{1,0:T(8,128)}), f32[96,768]{1,0:T(8,128)}) %reduce-scatter.16.cloned.1.call-update) | async-done | bytes 294928 | tf_op jit(solution)/shard_map/reduce_scatter | solution.py:219
  693.1 70.3 %reduce-scatter.18.cloned.1.call-done = f32[768,96]{0,1:T(8,128)} async-done(((f32[768,768]{0,1:T(8,128)}), f32[768,96]{0,1:T(8,128)}) %reduce-scatter.18.cloned.1.call-update) | async-done | bytes 294928 | tf_op jit(solution)/shard_map/reduce_scatter | solution.py:220
  772.3 60.7 %reduce-scatter.20.cloned.1.call-done = f32[96,576]{1,0:T(8,128)} async-done(((f32[768,576]{1,0:T(8,128)}), f32[96,576]{1,0:T(8,128)}) %reduce-scatter.20.cloned.1.call-update) | async-done | bytes 221200
  849.6 39.7 %psum.39 = f32[2,15]{1,0:T(2,128)S(1)} all-reduce(f32[2,15]{1,0:T(2,128)S(1)} %pad_maximum_fusion.3), channel_id=1, replica_groups=mesh['dp'=8,'tensor'=4] {'dp','tensor'}, use_global_device_ids=true, to_apply=%region_67.68 | all-reduce | flops 30 | bytes 240 | tf_op jit(solution)/shard_map/psum | solution.py:272
  (339 shorter events, 248.9 us)
Async XLA Ops:
  8.0 201.7 %all-reduce.9.cloned.1.call-start = ((), (), s32[]{:S(2)}) async-start(), calls=%async_computation.6 | async-start | bytes 6291456 | tf_op jit(solution)/shard_map/psum | solution.py:154
  105.0 104.7 %copy-start = (bf16[2048,768]{1,0:T(8,128)(2,1)S(1)}, bf16[2048,768]{1,0:T(8,128)(2,1)}, u32[]{:S(2)}) copy-start(bf16[2048,768]{1,0:T(8,128)(2,1)} %param.33) | copy-start | bytes 9437188
  143.8 71.4 %all-gather.6.cloned.1.call-start = ((), (), s32[]{:S(2)}) async-start(), calls=%async_computation.7 | async-start | bytes 1327104 | tf_op jit(solution)/shard_map/all_gather | solution.py:132
  145.5 90.3 %all-gather.8.cloned.1.call-start = ((), (), s32[]{:S(2)}) async-start(), calls=%async_computation.8 | async-start | bytes 1327104 | tf_op jit(solution)/shard_map/all_gather | solution.py:133
  147.3 163.8 %all-reduce.11.cloned.1.call-start = ((), (), s32[]{:S(2)}) async-start(), calls=%async_computation.9 | async-start | bytes 6291456 | tf_op jit(solution)/shard_map/psum | solution.py:165
  242.3 166.7 %all-reduce.13.cloned.1.call-start = ((), (), s32[]{:S(2)}) async-start(), calls=%async_computation.10 | async-start | bytes 6291456 | tf_op jit(solution)/shard_map/psum | solution.py:182
  340.3 251.6 %reduce-scatter.24.cloned.1.call-start = ((), (), s32[]{:S(2)}) async-start(), calls=%async_computation.16 | async-start | bytes 442368
  428.5 166.9 %reduce-scatter.26.cloned.1.call-start = ((), (), s32[]{:S(2)}) async-start(), calls=%async_computation.17 | async-start | bytes 442368
  431.5 187.7 %reduce-scatter.22.cloned.1.call-start = ((), (), s32[]{:S(2)}) async-start(), calls=%async_computation.15 | async-start | bytes 884736
  437.3 254.0 %reduce-scatter.16.cloned.1.call-start = ((), (), s32[]{:S(2)}) async-start(), calls=%async_computation.12 | async-start | bytes 2654208 | tf_op jit(solution)/shard_map/reduce_scatter | solution.py:219
  445.1 318.3 %reduce-scatter.18.cloned.1.call-start = ((), (), s32[]{:S(2)}) async-start(), calls=%async_computation.13 | async-start | bytes 2654208 | tf_op jit(solution)/shard_map/reduce_scatter | solution.py:220
  453.0 380.0 %reduce-scatter.20.cloned.1.call-start = ((), (), s32[]{:S(2)}) async-start(), calls=%async_computation.14 | async-start | bytes 2211840
  547.8 295.7 %all-reduce.15.cloned.1.call-start = ((), (), s32[]{:S(2)}) async-start(), calls=%async_computation.11 | async-start | bytes 6291456 | tf_op jit(solution)/shard_map/psum | solution.py:212
  583.9 107.5 %copy-start.12 = (f32[96,768]{1,0:T(8,128)S(1)}, f32[96,768]{1,0:T(8,128)}, u32[]{:S(2)}) copy-start(f32[96,768]{1,0:T(8,128)} %param.44) | copy-start | bytes 884740
  583.9 107.4 %copy-start.22 = (f32[96,768]{1,0:T(8,128)S(1)}, f32[96,768]{1,0:T(8,128)}, u32[]{:S(2)}) copy-start(f32[96,768]{1,0:T(8,128)} %param.46) | copy-start | bytes 884740
  583.9 107.4 %copy-start.23 = (f32[96,768]{1,0:T(8,128)S(1)}, f32[96,768]{1,0:T(8,128)}, u32[]{:S(2)}) copy-start(f32[96,768]{1,0:T(8,128)} %param.45) | copy-start | bytes 884740
  583.9 179.5 %copy-start.11 = (f32[768,96]{0,1:T(8,128)S(1)}, f32[768,96]{0,1:T(8,128)}, u32[]{:S(2)}) copy-start(f32[768,96]{0,1:T(8,128)} %param.47) | copy-start | bytes 884740
  583.9 179.5 %copy-start.24 = (f32[768,96]{0,1:T(8,128)S(1)}, f32[768,96]{0,1:T(8,128)}, u32[]{:S(2)}) copy-start(f32[768,96]{0,1:T(8,128)} %param.49) | copy-start | bytes 884740
  621.5 279.2 %copy-start.20 = (f32[192,96]{1,0:T(8,128)}, f32[192,96]{1,0:T(8,128)S(1)}, u32[]{:S(2)}) copy-start(f32[192,96]{1,0:T(8,128)S(1)} %get-tuple-element.444) | copy-start | bytes 221188
  693.1 206.8 %copy-start.14 = (f32[96,768]{1,0:T(8,128)}, f32[96,768]{1,0:T(8,128)S(1)}, u32[]{:S(2)}) copy-start(f32[96,768]{1,0:T(8,128)S(1)} %get-tuple-element.442) | copy-start | bytes 884740
  693.1 206.8 %copy-start.15 = (f32[96,768]{1,0:T(8,128)}, f32[96,768]{1,0:T(8,128)S(1)}, u32[]{:S(2)}) copy-start(f32[96,768]{1,0:T(8,128)S(1)} %get-tuple-element.443) | copy-start | bytes 884740
  843.5 55.6 %copy-start.16 = (f32[768,96]{0,1:T(8,128)S(1)}, f32[768,96]{0,1:T(8,128)}, u32[]{:S(2)}) copy-start(f32[768,96]{0,1:T(8,128)} %get-tuple-element.440) | copy-start | bytes 884740
  843.5 55.6 %copy-start.17 = (f32[768,96]{0,1:T(8,128)S(1)}, f32[768,96]{0,1:T(8,128)}, u32[]{:S(2)}) copy-start(f32[768,96]{0,1:T(8,128)} %get-tuple-element.441) | copy-start | bytes 884740
  843.5 57.3 %copy-start.21 = (f32[192,96]{1,0:T(8,128)S(1)}, f32[192,96]{1,0:T(8,128)}, u32[]{:S(2)}) copy-start(f32[192,96]{1,0:T(8,128)} %get-tuple-element.445) | copy-start | bytes 221188
  (49 other events, 654.3 us)
Sparse Core Ops, SparseCore 0:
  143.9 65.7 all-reduce.8
  242.5 68.5 all-reduce.10
  340.4 68.5 all-reduce.12
  590.7 64.9 all-reduce.14
Sparse Core Ops, SparseCore 1:
  147.0 38.5 all-gather.5
  188.2 40.1 all-gather.7
  428.6 61.6 reduce-scatter.23
  493.5 60.6 reduce-scatter.25
  557.5 61.6 reduce-scatter.21
  623.1 68.1 reduce-scatter.15
  695.1 68.2 reduce-scatter.17
  767.1 65.8 reduce-scatter.19
where the time goes:
time: 916 us; the launch traced here: 909 us
  waiting for transfers between devices  356 us (39%)
  blocking collectives  203 us (22%)
  matrix products  136 us (15%)
  local copies, waits for them, and re-layouts  98.6 us (11%)
  other arithmetic  85.6 us (9%)
  between operations  28.7 us (3%)
    unnamed x16, waiting for transfers between devices  80.1 us
    reduce_scatter x1, waiting for transfers between devices, on_device(): lax.psum_scatter(down_grad, 'dp', scatter_dimension=1, tiled=True)  70.3 us
    reduce_scatter x1, waiting for transfers between devices, on_device(): lax.psum_scatter(up_grad, 'dp', scatter_dimension=0, tiled=True)  69.8 us
    psum x1, waiting for transfers between devices, on_device(): lax.psum(ffn_part.astype(jnp.bfloat16), 'tensor').astype(jnp.float32)  68.4 us
    psum x1, waiting for transfers between devices, on_device(): lax.psum(normed_part.astype(jnp.bfloat16), 'tensor').astype(jnp.float32)  66.1 us
    psum x1, blocking collectives, on_device(): lax.psum(jnp.stack([jnp.stack(weight_sq), jnp.stack(update_sq)]), ('dp',...  39.7 us
    unnamed x2, blocking collectives  39.4 us
    all_gather x1, blocking collectives, on_device(): lax.all_gather(attn_weight.astype(bfloat), 'dp', axis=1, tiled=True)  38.6 us
  transfers between devices with their start and end apart: 12, of which 7 were waited for; matrix products, arithmetic and copies ran while one was open for 22% of the time, Pallas kernels for 0%

commit v1 on v0

v1 whole, which is shorter than its diff:
```python
import functools

import jax
import jax.numpy as jnp
from jax import lax
from jax.experimental import pallas as pl
from jax.experimental.pallas import tpu as pltpu
from jax.sharding import PartitionSpec as P

HEAD = 64
BF = jnp.bfloat16
F32 = jnp.float32
NN = (((1,), (0,)), ((), ()))
NT = (((1,), (1,)), ((), ()))
TN = (((0,), (0,)), ((), ()))


def mm(a, b, dims):
    return lax.dot_general(a, b, dims, preferred_element_type=F32)


class GenericComm:
    def __init__(self, dp, tensor):
        self.dp, self.tensor = dp, tensor

    def gather(self, shard):
        rows = lax.all_gather(shard, "dp", axis=0, tiled=True)
        return lax.all_gather(rows, "tensor", axis=0)

    def scatter(self, blocks):
        stacked = jnp.stack(blocks)
        own = lax.psum_scatter(stacked, "tensor", scatter_dimension=0)
        return lax.psum_scatter(own, "dp", scatter_dimension=0, tiled=True).astype(F32)

    def gather_small(self, vector):
        return lax.all_gather(lax.all_gather(vector, "dp", axis=0), "tensor", axis=0)

    def scatter_small(self, vectors):
        own = lax.psum_scatter(vectors, "tensor", scatter_dimension=0)
        return lax.psum_scatter(own, "dp", scatter_dimension=0)

    def total(self, values):
        return lax.psum(values, ("dp", "tensor"))

    def gather_rows(self, rows):
        return lax.all_gather(rows, "tensor", axis=0, tiled=True)


class GridComm:
    def __init__(self):
        self.z = lax.axis_index("dp") // 2
        self.y = lax.axis_index("dp") % 2

    @staticmethod
    def send(array, dp_xor, tensor_xor):
        pairs = [
            (d * 4 + t, (d ^ dp_xor) * 4 + (t ^ tensor_xor)) for d in range(8) for t in range(4)
        ]
        return lax.ppermute(array, ("dp", "tensor"), pairs)

    def send_core(self, array):
        return self.send(array, 0, 1)

    def send_x(self, array):
        return self.send(array, 0, 2)

    def send_y(self, array):
        return self.send(array, 1, 0)

    def send_z(self, array, k):
        return self.send(array, 2 * k, 0)

    def gather_pieces(self, shard):
        own = jnp.stack([shard] + [self.send_z(shard, k) for k in (1, 2, 3)])
        from_x = self.send_x(own)
        from_y = self.send_y(own)
        diag_low = self.send_x(from_y[:2])
        diag_high = self.send_y(from_x[2:])
        near = [own, from_y]
        far = [from_x, diag_low, diag_high]
        return [
            near,
            [self.send_core(a) for a in near],
            far,
            [self.send_core(a) for a in far],
        ]

    def gather(self, shard):
        pieces = self.gather_pieces(shard)
        return place(pieces, self.z, self.y, shard.shape)

    def split(self, block):
        view = block.reshape(4, 2, block.shape[0] // 8, block.shape[1])
        own = lax.dynamic_index_in_dim(view, self.y, 1, keepdims=False)
        other = lax.dynamic_index_in_dim(view, 1 - self.y, 1, keepdims=False)
        return own, other

    def scatter(self, blocks):
        near_own, near_other = self.split(blocks[0])
        far_own, far_other = self.split(blocks[2])
        near_got = self.send_core(blocks[1])
        far_got = self.send_core(blocks[3])
        near_got_own, near_got_other = self.split(near_got)
        far_got_own, far_got_other = self.split(far_got)
        diag = add(far_other, far_got_other)
        diag_low = self.send_x(diag[:2])
        diag_high = self.send_y(diag[2:])
        zeros = jnp.zeros_like(diag_low)
        to_y = add(near_other, near_got_other, jnp.concatenate([diag_low, zeros]))
        to_x = add(far_own, far_got_own, jnp.concatenate([zeros, diag_high]))
        from_x = self.send_x(to_x)
        from_y = self.send_y(to_y)
        own = add(near_own, near_got_own, from_x, from_y)
        parts = [lax.dynamic_index_in_dim(own, self.z ^ k, 0, keepdims=False) for k in range(4)]
        total = parts[0].astype(F32)
        for k in (1, 2, 3):
            total = total + self.send_z(parts[k], k).astype(F32)
        return total

    def gather_small(self, vector):
        own = jnp.stack([vector] + [self.send_z(vector, k) for k in (1, 2, 3)])
        own = jnp.stack([own, self.send_y(own)], axis=1)
        own = jnp.stack([own, self.send_x(own)])
        own = jnp.stack([own, self.send_core(own)], axis=1)
        own = own.reshape((4, 2, 2, 2) + vector.shape)
        own = swap_if(self.z >= 2, own, 1)
        own = swap_if(self.z % 2 == 1, own, 2)
        own = swap_if(self.y == 1, own, 3)
        return own.reshape((4, 8) + vector.shape)

    def scatter_small(self, vectors):
        shape = vectors.shape[2:]
        near = vectors[0::2] + self.send_core(vectors[1::2])
        own = near[0] + self.send_x(near[1])
        own = own.reshape((4, 2) + shape)
        mine = lax.dynamic_index_in_dim(own, self.y, 1, keepdims=False)
        other = lax.dynamic_index_in_dim(own, 1 - self.y, 1, keepdims=False)
        mine = mine + self.send_y(other)
        parts = [lax.dynamic_index_in_dim(mine, self.z ^ k, 0, keepdims=False) for k in range(4)]
        total = parts[0]
        for k in (1, 2, 3):
            total = total + self.send_z(parts[k], k)
        return total

    def total(self, values):
        values = values + self.send_core(values)
        values = values + self.send_x(values)
        values = values + self.send_y(values)
        values = values + self.send_z(values, 1)
        return values + self.send_z(values, 2)

    def gather_rows(self, rows):
        far = self.send_x(rows)
        pieces = [rows, self.send_core(rows), far, self.send_core(far)]
        return place_rows(pieces, lax.axis_index("tensor"))


def swap_if(flag, array, axis):
    return jnp.where(flag, jnp.flip(array, axis), array)


def place_rows(pieces, rank):
    n = pieces[0].shape[0]

    def kernel(rank_ref, *refs):
        out_ref, sems = refs[len(pieces)], refs[len(pieces) + 1]
        copies = [
            pltpu.make_async_copy(refs[p], out_ref.at[rank_ref[0] ^ p], sems.at[p])
            for p in range(len(pieces))
        ]
        for copy in copies:
            copy.start()
        for copy in copies:
            copy.wait()

    out = pl.pallas_call(
        kernel,
        out_shape=jax.ShapeDtypeStruct((len(pieces),) + pieces[0].shape, pieces[0].dtype),
        in_specs=[pl.BlockSpec(memory_space=pltpu.SMEM)]
        + [pl.BlockSpec(memory_space=pl.ANY)] * len(pieces),
        out_specs=pl.BlockSpec(memory_space=pl.ANY),
        scratch_shapes=[pltpu.SemaphoreType.DMA((len(pieces),))],
        cost_estimate=pl.CostEstimate(flops=0, bytes_accessed=8 << 20, transcendentals=0),
    )(rank.reshape(1).astype(jnp.int32), *pieces)
    return out.reshape((len(pieces) * n,) + pieces[0].shape[1:])


def add(*arrays):
    total = arrays[0].astype(F32)
    for array in arrays[1:]:
        total = total + array.astype(F32)
    return total.astype(BF)


def place(pieces, z, y, shard_shape):
    flat = [array for group in pieces for array in group]
    plan = []
    index = 0
    for p, group in enumerate(pieces):
        chunk = 0
        for array in group:
            for offset in range(array.shape[0]):
                plan.append((index, offset, p, chunk // 4, chunk % 4))
                chunk += 1
            index += 1

    def kernel(where_ref, *refs):
        sources, out_ref, sems = refs[: len(flat)], refs[len(flat)], refs[len(flat) + 1]
        z_at, y_at = where_ref[0], where_ref[1]
        copies = []
        for number, (source, offset, p, y_rel, z_rel) in enumerate(plan):
            row = (z_at ^ z_rel) * 2 + (y_at ^ y_rel)
            copies.append(
                pltpu.make_async_copy(
                    sources[source].at[offset], out_ref.at[p, row], sems.at[number]
                )
            )
        for copy in copies:
            copy.start()
        for copy in copies:
            copy.wait()

    out = pl.pallas_call(
        kernel,
        out_shape=jax.ShapeDtypeStruct((len(pieces), 8) + tuple(shard_shape), BF),
        in_specs=[pl.BlockSpec(memory_space=pltpu.SMEM)]
        + [pl.BlockSpec(memory_space=pl.ANY)] * len(flat),
        out_specs=pl.BlockSpec(memory_space=pl.ANY),
        scratch_shapes=[pltpu.SemaphoreType.DMA((len(plan),))],
        cost_estimate=pl.CostEstimate(flops=0, bytes_accessed=10 << 20, transcendentals=0),
    )(jnp.stack([z, y]).astype(jnp.int32), *flat)
    return out.reshape(len(pieces), 8 * shard_shape[0], shard_shape[1])


def attn_fwd_kernel(
    tok_ref, w_ref, bias_ref, gq_ref, gk_ref, open_ref,
    qkv_ref, ctx_ref, e_ref, inv_ref, att_ref, mask_ref,
):
    step = pl.program_id(0)
    width = ctx_ref.shape[2]

    @pl.when(step == 0)
    def _():
        seen = (open_ref[...] == 1) | (gq_ref[...] == gk_ref[...])
        mask_ref[...] = jnp.where(seen, 0.0, -1e30)
        att_ref[...] = jnp.zeros_like(att_ref)

    qkv = mm(tok_ref[...], w_ref[0, :, : 3 * width], NN)
    qkv = (qkv + bias_ref[0]).astype(BF)
    qkv_ref[0] = qkv
    lane = lax.broadcasted_iota(jnp.int32, (qkv.shape[0], 128), 1)
    contexts = []
    inv_all = jnp.zeros((qkv.shape[0], 128), F32)
    for h in range(width // HEAD):
        q = qkv[:, h * HEAD : (h + 1) * HEAD] * jnp.asarray(HEAD**-0.5, BF)
        k = qkv[:, width + h * HEAD : width + (h + 1) * HEAD]
        v = qkv[:, 2 * width + h * HEAD : 2 * width + (h + 1) * HEAD]
        s = mm(q, k, NT) + mask_ref[...]
        e = jnp.exp(s - jnp.max(s, axis=-1, keepdims=True)).astype(BF)
        e_ref[0, h] = e
        v_one = jnp.concatenate([v, jnp.ones_like(v)], axis=1)
        r = mm(e, v_one, NN)
        inv = 1.0 / r[:, HEAD : HEAD + 1]
        contexts.append((r[:, :HEAD] * inv).astype(BF))
        inv_all = jnp.where(lane == h, inv, inv_all)
    ctx = jnp.concatenate(contexts, axis=1)
    ctx_ref[0] = ctx
    inv_ref[0] = inv_all
    att_ref[...] += mm(ctx, w_ref[0, :, 3 * width :], NT)


def attn_fwd(tok, w, bias, groups, key_open):
    blocks, d, wide = w.shape
    n = tok.shape[0]
    width = wide // 4
    heads = width // HEAD
    full = lambda *s: pl.BlockSpec(s, lambda i: (0,) * len(s))
    per = lambda *s: pl.BlockSpec((1,) + s, lambda i: (i,) + (0,) * len(s))
    return pl.pallas_call(
        attn_fwd_kernel,
        grid=(blocks,),
        in_specs=[
            full(n, d), per(d, wide), per(1, 3 * width), full(n, 1), full(1, n), full(1, n),
        ],
        out_specs=[
            per(n, 3 * width), per(n, width), per(heads, n, n), per(n, 128), full(n, d),
        ],
        out_shape=[
            jax.ShapeDtypeStruct((blocks, n, 3 * width), BF),
            jax.ShapeDtypeStruct((blocks, n, width), BF),
            jax.ShapeDtypeStruct((blocks, heads, n, n), BF),
            jax.ShapeDtypeStruct((blocks, n, 128), F32),
            jax.ShapeDtypeStruct((n, d), F32),
        ],
        scratch_shapes=[pltpu.VMEM((n, n), F32)],
        compiler_params=pltpu.CompilerParams(vmem_limit_bytes=40 << 20),
        cost_estimate=pl.CostEstimate(
            flops=14 << 30, bytes_accessed=16 << 20, transcendentals=12 * n * n
        ),
    )(tok, w, bias, groups.reshape(n, 1), groups.reshape(1, n), key_open.reshape(1, n))


def attn_bwd_kernel(
    da_ref, w_ref, qkv_ref, ctx_ref, e_ref, inv_ref, ds1_ref, dqkv_ref, sum_ref, tg_ref
):
    step = pl.program_id(0)
    width = ctx_ref.shape[2]

    @pl.when(step == 0)
    def _():
        tg_ref[...] = ds1_ref[...]

    dctx = mm(da_ref[...], w_ref[0, :, 3 * width :], NN).astype(BF).astype(F32)
    scale = HEAD**-0.5
    dqs, dks, dvs = [], [], []
    for h in range(width // HEAD):
        q = qkv_ref[0, :, h * HEAD : (h + 1) * HEAD]
        k = qkv_ref[0, :, width + h * HEAD : width + (h + 1) * HEAD]
        v = qkv_ref[0, :, 2 * width + h * HEAD : 2 * width + (h + 1) * HEAD]
        e = e_ref[0, h]
        inv = inv_ref[0, :, h : h + 1]
        do = dctx[:, h * HEAD : (h + 1) * HEAD] * inv
        ctx = ctx_ref[0, :, h * HEAD : (h + 1) * HEAD].astype(F32)
        delta = jnp.sum(do * ctx, axis=-1, keepdims=True)
        do_low = do.astype(BF)
        dp = mm(do_low, v, NT)
        ds = (e.astype(F32) * (dp - delta)).astype(BF)
        dvs.append(mm(e, do_low, TN))
        dqs.append(mm(ds, k, NN) * scale)
        dks.append(mm(ds, q, TN) * scale)
    dqkv = jnp.concatenate(dqs + dks + dvs, axis=1).astype(BF)
    dqkv_ref[0] = dqkv
    sum_ref[0] = jnp.sum(dqkv.astype(F32), axis=0, keepdims=True)
    tg_ref[...] += mm(dqkv, w_ref[0, :, : 3 * width], NT)


def attn_bwd(da, w, qkv, ctx, e, inv, ds1):
    blocks, d, wide = w.shape
    n = da.shape[0]
    width = wide // 4
    heads = width // HEAD
    full = lambda *s: pl.BlockSpec(s, lambda i: (0,) * len(s))
    per = lambda *s: pl.BlockSpec((1,) + s, lambda i: (i,) + (0,) * len(s))
    return pl.pallas_call(
        attn_bwd_kernel,
        grid=(blocks,),
        in_specs=[
            full(n, d), per(d, wide), per(n, 3 * width), per(n, width), per(heads, n, n),
            per(n, 128), full(n, d),
        ],
        out_specs=[per(n, 3 * width), per(1, 3 * width), full(n, d)],
        out_shape=[
            jax.ShapeDtypeStruct((blocks, n, 3 * width), BF),
            jax.ShapeDtypeStruct((blocks, 1, 3 * width), F32),
            jax.ShapeDtypeStruct((n, d), F32),
        ],
        compiler_params=pltpu.CompilerParams(vmem_limit_bytes=40 << 20),
        cost_estimate=pl.CostEstimate(
            flops=20 << 30, bytes_accessed=16 << 20, transcendentals=0
        ),
    )(da, w, qkv, ctx, e, inv, ds1)


def layer_norm(summed):
    center = summed - jnp.mean(summed, axis=-1, keepdims=True)
    spread = jnp.mean(center * center, axis=-1, keepdims=True)
    scaled = lax.rsqrt(spread + 1e-05)
    return (center * scaled, scaled)


def norm_back(upstream, normal, scaled):
    inner_sum = (
        upstream
        - jnp.mean(upstream, axis=-1, keepdims=True)
        - normal * jnp.mean(upstream * normal, axis=-1, keepdims=True)
    )
    return scaled * inner_sum


def square_sums(array, piece_count, weight_factor):
    if piece_count == 1:
        return [jnp.sum(array * array) * weight_factor]
    return [jnp.sum(array[member] * array[member]) * weight_factor for member in range(piece_count)]


def trust_factor(trust, offset, piece_count, rank_count):
    if piece_count == 1:
        return trust[offset]
    return trust[offset : offset + piece_count].reshape((piece_count,) + (1,) * (rank_count - 1))


def on_device(
    dp_size, tensor_size,
    tokens, cotangent, row_lengths, present, groups,
    attn_weight, attn_first, attn_second,
    mix_weight, mix_first, mix_second,
    up_weight, up_first, up_second,
    down_weight, down_first, down_second,
    head_bias, head_first, head_second,
    wide_bias, wide_first, wide_second,
    norm_gains, gain_first, gain_second,
    shift_bias, shift_first, shift_second,
):
    comm = GridComm() if (dp_size, tensor_size) == (8, 4) else GenericComm(dp_size, tensor_size)
    rank = lax.axis_index("tensor")
    row_count, n = groups.shape
    assert row_count == tensor_size
    d = tokens.shape[1]
    width = attn_weight.shape[2]
    head_own, wide_own, gain_own = head_bias.shape[1], wide_bias.shape[0], norm_gains.shape[1]

    attn_shard = jnp.concatenate(
        [attn_weight[0], attn_weight[1], attn_weight[2], mix_weight.T], axis=1
    ).astype(BF)
    up_shard = up_weight.astype(BF)
    down_shard = down_weight.T.astype(BF)
    small = jnp.concatenate(
        [head_bias.reshape(-1), wide_bias, norm_gains.reshape(-1), shift_bias.reshape(-1)]
    )
    small = small.astype(BF).astype(F32)
    cuts = (2 * head_own, wide_own, 2 * gain_own, 4 * gain_own)
    pad = -sum(cuts) % 1024
    small = jnp.pad(small, (0, pad)).reshape(-1, 128)

    small_all = comm.gather_small(small).reshape(tensor_size, dp_size, -1)
    attn_all = comm.gather(attn_shard)
    up_all = comm.gather(up_shard)
    down_all = comm.gather(down_shard)

    at = [0, cuts[0], cuts[0] + cuts[1], cuts[0] + cuts[1] + cuts[2], sum(cuts)]
    heads_low = small_all[:, :, at[0] : at[1]].reshape(tensor_size, dp_size, 2, head_own)
    heads_low = heads_low.transpose(0, 2, 1, 3).reshape(tensor_size, 2, width)
    wide_low = small_all[:, :, at[1] : at[2]].reshape(tensor_size, 1, -1)
    gains = small_all[0, :, at[2] : at[3]].reshape(dp_size, 2, gain_own)
    gains = gains.transpose(1, 0, 2).reshape(2, d)
    shifts = small_all[0, :, at[3] : at[4]].reshape(dp_size, 4, gain_own)
    shifts = shifts.transpose(1, 0, 2).reshape(4, d)

    tok = lax.dynamic_slice_in_dim(tokens, rank * n, n, 0)
    cot = lax.dynamic_slice_in_dim(cotangent, rank * n, n, 0)
    group_row = lax.dynamic_index_in_dim(groups, rank, 0, keepdims=False)
    present_row = lax.dynamic_index_in_dim(present, rank, 0, keepdims=False)
    length = lax.dynamic_index_in_dim(row_lengths, rank, 0, keepdims=False)
    feature_ids = jnp.arange(present_row.shape[0])
    present_key = jnp.sum(
        (group_row[:, None] == feature_ids[None, :]) * present_row[None, :], axis=1
    )
    key_open = ((jnp.arange(n) < length) & (present_key == 1)).astype(jnp.int32)

    qkv_bias = jnp.concatenate(
        [heads_low[:, :1], jnp.zeros_like(heads_low[:, :1]), heads_low[:, 1:]], axis=2
    )
    qkv, ctx, e, inv, attended = attn_fwd(tok, attn_all, qkv_bias, group_row, key_open)
    normal_one, scaled_one = layer_norm(tok.astype(F32) + attended + shifts[0])
    normed = normal_one * gains[0] + shifts[1]
    normed_low = normed.astype(BF)
    hidden = jnp.einsum("td,pdf->ptf", normed_low, up_all, preferred_element_type=F32) + wide_low
    active, gelu_back = jax.vjp(functools.partial(jax.nn.gelu, approximate=False), hidden)
    active_low = active.astype(BF)
    mixed = jnp.einsum("ptf,pdf->td", active_low, down_all, preferred_element_type=F32)
    normal_two, scaled_two = layer_norm(normed + mixed + shifts[2])
    layer_out = (normal_two * gains[1] + shifts[3]).astype(BF)
    layer_out_all = comm.gather_rows(layer_out)
    upstream = cot.astype(F32)
    gain_two_grad = jnp.sum(upstream * normal_two, axis=0)
    shift_three_grad = jnp.sum(upstream, axis=0)
    back_two = norm_back(upstream * gains[1], normal_two, scaled_two)
    shift_two_grad = jnp.sum(back_two, axis=0)
    df = back_two.astype(BF)
    down_grads = [mm(df, active_low[p], TN).astype(BF) for p in range(tensor_size)]
    down_sum = comm.scatter(down_grads)
    active_grad = jnp.einsum("td,pdf->ptf", df, down_all, preferred_element_type=F32)
    dh = gelu_back(active_grad)[0].astype(BF)
    wide_grad = jnp.sum(dh.astype(F32), axis=1)
    up_grads = [mm(normed_low, dh[p], TN).astype(BF) for p in range(tensor_size)]
    up_sum = comm.scatter(up_grads)
    normed_grad = back_two + jnp.einsum("ptf,pdf->td", dh, up_all, preferred_element_type=F32)
    gain_one_grad = jnp.sum(normed_grad * normal_one, axis=0)
    shift_one_grad = jnp.sum(normed_grad, axis=0)
    back_one = norm_back(normed_grad * gains[0], normal_one, scaled_one)
    shift_zero_grad = jnp.sum(back_one, axis=0)
    da = back_one.astype(BF)
    dqkv, dqkv_sum, tokens_grad = attn_bwd(da, attn_all, qkv, ctx, e, inv, back_one)
    tokens_grad_all = comm.gather_rows(tokens_grad.astype(BF))
    attn_grads = [
        jnp.concatenate([mm(tok, dqkv[p], TN), mm(da, ctx[p], TN)], axis=1).astype(BF)
        for p in range(tensor_size)
    ]
    attn_sum = comm.scatter(attn_grads)

    head_grad = jnp.stack([dqkv_sum[:, 0, :width], dqkv_sum[:, 0, 2 * width :]], axis=1)
    head_grad = head_grad.reshape(tensor_size, 2, dp_size, head_own).transpose(0, 2, 1, 3)
    wide_part = wide_grad.reshape(tensor_size, dp_size, wide_own)
    vectors = jnp.stack(
        [
            gain_one_grad, gain_two_grad,
            shift_zero_grad, shift_one_grad, shift_two_grad, shift_three_grad,
        ]
    )
    vectors = vectors.reshape(6, dp_size, gain_own).transpose(1, 0, 2).reshape(1, dp_size, -1)
    small_grad = jnp.concatenate(
        [
            head_grad.reshape(tensor_size, dp_size, -1),
            wide_part,
            jnp.broadcast_to(vectors, (tensor_size,) + vectors.shape[1:]),
        ],
        axis=2,
    )
    small_grad = jnp.pad(small_grad, ((0, 0), (0, 0), (0, pad)))
    small_sum = comm.scatter_small(
        small_grad.reshape((tensor_size, dp_size) + small.shape)
    ).reshape(-1)

    reduced = (
        jnp.stack([attn_sum[:, k * width : (k + 1) * width] for k in range(3)]),
        attn_sum[:, 3 * width :].T,
        up_sum,
        down_sum.T,
        small_sum[at[0] : at[1]].reshape(head_bias.shape),
        small_sum[at[1] : at[2]],
        small_sum[at[2] : at[3]].reshape(norm_gains.shape),
        small_sum[at[3] : at[4]].reshape(shift_bias.shape),
    )
    masters = (
        attn_weight, mix_weight, up_weight, down_weight,
        head_bias, wide_bias, norm_gains, shift_bias,
    )
    firsts = (
        attn_first, mix_first, up_first, down_first,
        head_first, wide_first, gain_first, shift_first,
    )
    seconds = (
        attn_second, mix_second, up_second, down_second,
        head_second, wide_second, gain_second, shift_second,
    )
    piece_counts = (3, 1, 1, 1, 2, 1, 2, 4)
    share = 1.0 / tensor_size
    weight_factors = (1.0, 1.0, 1.0, 1.0, 1.0, 1.0, share, share)
    new_firsts, new_seconds, updates, weight_sq, update_sq = ([], [], [], [], [])
    for master, first_old, second_old, gradient, piece_count, weight_factor in zip(
        masters, firsts, seconds, reduced, piece_counts, weight_factors
    ):
        first_new = 0.5 * first_old + 0.5 * gradient
        second_new = 0.5 * second_old + 0.5 * gradient * gradient
        update = first_new / (jnp.sqrt(second_new) + 1e-06) + 0.01 * master
        new_firsts.append(first_new)
        new_seconds.append(second_new)
        updates.append(update)
        weight_sq.extend(square_sums(master, piece_count, weight_factor))
        update_sq.extend(square_sums(update, piece_count, weight_factor))
    square_totals = comm.total(jnp.stack([jnp.stack(weight_sq), jnp.stack(update_sq)]))
    norm_pairs = jnp.sqrt(square_totals)
    trust = norm_pairs[0] / (norm_pairs[1] + 1e-06)
    out = [layer_out_all, tokens_grad_all]
    offset = 0
    for index, (master, update, piece_count) in enumerate(zip(masters, updates, piece_counts)):
        factor = trust_factor(trust, offset, piece_count, master.ndim)
        out.extend([master - 0.5 * factor * update, new_firsts[index], new_seconds[index]])
        offset = offset + piece_count
    return tuple(out) + (norm_pairs,)


def solution(mesh):
    rows = P("dp", None)
    attn, mix, up = P(None, "dp", "tensor"), P("tensor", "dp"), P("dp", "tensor")
    head, wide, col = P(None, ("tensor", "dp")), P(("tensor", "dp")), P(None, "dp")
    params = tuple(spec for spec in (attn, mix, up, mix, head, wide, col, col) for _ in range(3))
    return jax.shard_map(
        functools.partial(on_device, mesh.shape["dp"], mesh.shape["tensor"]),
        mesh=mesh,
        in_specs=(rows, rows, P("dp"), rows, rows) + params,
        out_specs=(rows, rows) + params + (P(),),
        check_vma=False,
    )
```

time: 916 us -> 1050 us (1.15)
  Pallas kernels: 0 us -> 659 us
  waiting for transfers between devices: 356 us -> 120 us
  blocking collectives: 203 us -> 0 us
  starting transfers between devices: 1.13 us -> 80.3 us
  matrix products: 136 us -> 63.7 us
  local copies, waits for them, and re-layouts: 98.6 us -> 50.9 us
  other arithmetic: 85.6 us -> 60.6 us
  between operations: 28.7 us -> 12.6 us
    pallas_call x0 -> x7, Pallas kernels: none -> 659 us  [the longest x3 435 us: place(): pl.pallas_call(kernel, out_shape=jax.ShapeDtypeStruct((len(pieces), 8) +...]
    reduce_scatter x2 -> x0, waiting for transfers between devices: 140 us -> none  [the longest x1 70.3 us: on_device(): lax.psum_scatter(down_grad, 'dp', scatter_dimension=1, tiled=True)]
    psum x4 -> x0, waiting for transfers between devices: 136 us -> none  [the longest x1 68.4 us: on_device(): lax.psum(ffn_part.astype(jnp.bfloat16), 'tensor').astype(jnp.float32)]
    all_gather x5 -> x0, blocking collectives: 124 us -> none  [the longest x1 38.6 us: on_device(): lax.all_gather(attn_weight.astype(bfloat), 'dp', axis=1, tiled=True)]
    ppermute x0 -> x86, waiting for transfers between devices: none -> 120 us  [send(): return lax.ppermute(array, ('dp', 'tensor'), pairs)]
    ppermute x0 -> x86, starting transfers between devices: none -> 80.3 us  [send(): return lax.ppermute(array, ('dp', 'tensor'), pairs)]
    unnamed x16 -> x0, waiting for transfers between devices: 80.1 us -> none
    dot_general x39 -> x20, matrix products: 131 us -> 63.7 us  [the longest x16 28.4 us: mm(): return lax.dot_general(a, b, dims, preferred_element_type=F32)]
  transfers between devices with their start and end apart: 12 -> 86, of which waited for: 7 -> 24; matrix products, arithmetic and copies ran while one was open for 22% -> 10% of each run, Pallas kernels for 0% -> 47%
where the time goes in v1:
time: 1050 us
  Pallas kernels  659 us (63%)
  waiting for transfers between devices  120 us (11%)
  starting transfers between devices  80.3 us (8%)
  matrix products  63.7 us (6%)
  other arithmetic  60.6 us (6%)
  local copies, waits for them, and re-layouts  50.9 us (5%)
  between operations  12.6 us (1%)
    pallas_call x3, Pallas kernels, place(): pl.pallas_call(kernel, out_shape=jax.ShapeDtypeStruct((len(pieces), 8) +...  435 us
    pallas_call x2, Pallas kernels, place_rows(): pl.pallas_call(kernel, out_shape=jax.ShapeDtypeStruct((len(pieces),) + pi...  193 us
    ppermute x86, waiting for transfers between devices, send(): return lax.ppermute(array, ('dp', 'tensor'), pairs)  120 us
    ppermute x86, starting transfers between devices, send(): return lax.ppermute(array, ('dp', 'tensor'), pairs)  80.3 us
    dot_general x16, matrix products, mm(): return lax.dot_general(a, b, dims, preferred_element_type=F32)  28.4 us
  transfers between devices with their start and end apart: 86, of which 24 were waited for; matrix products, arithmetic and copies ran while one was open for 10% of the time, Pallas kernels for 47%

profile of v1, /device:TPU:0, one launch (start us, length us, event | category | flops | bytes accessed | tf_op | source)
XLA Modules:
  0.0 1046.5 jit_solution(1796581763778421004)
XLA Ops:
  2.9 5.1 collective-permute-start.2
  75.1 4.9 collective-permute-done.24.refs_4_
  81.5 11.1 %collective-permute-done.36.refs_4_ = bf16[4,96,768]{2,1,0:T(8,128)(2,1)} collective-permute-done((bf16[4,96,768]{2,1,0:T(8,128)(2,1)}, bf16[4,96,768]{2,1,0:T(8,128)(2,1)}, u32[]{:S(2)}, u32[]{:S(2)}) %collective-permute-start.36) | collective-permute-done | bytes 589856 | tf_op jit(solution)/shard_map/ppermute | solution.py:59
  93.3 5.2 collective-permute-done.7.refs_5_
  110.0 145.0 %shard_map.484 = bf16[4,8,96,768]{3,2,1,0:T(8,128)(2,1)} custom-call(s32[2]{0:T(128)} %pad_add_fusion.where_ref, bf16[4,96,768]{2,1,0:T(8,128)(2,1)} %copy-done.22, bf16[4,96,768]{2,1,0:T(8,128)(2,1)} %collective-permute-done.3.refs_1_, bf16[4,96,768]{2,1,0:T(8,128)(2,1)} %copy-done.43, bf16[4,96,768]{2,1,0:T(8,128)(2,1)} %collective-permute-done.5.refs_3_, ...), custom_call_target="tpu_custom_call" | custom-call | bytes 10485760 | tf_op jit(solution)/shard_map/pallas_call | solution.py:223
  257.3 11.8 %shard_map.485 = (bf16[4,512,576]{2,1,0:T(8,128)(2,1)S(1)}, bf16[4,512,192]{2,1,0:T(8,128)(2,1)S(1)}, bf16[4,3,512,512]{3,2,1,0:T(8,128)(2,1)}, f32[4,512,128]{2,1,0:T(8,128)S(1)}, f32[512,768]{1,0:T(8,128)S(1)}) custom-call(bf16[512,768]{1,0:T(8,128)(2,1)S(1)} %constant_dynamic-slice_fusion.8.tok_ref, bf16[4,768,768]{2,1,0:T(8,128)(2,1)S(1)} %bitcast.481, ...), custom_call_target="tpu_custom_call" | custom-call | flops 15032385536 | bytes 16777216 | tf_op jit(solution)/shard_map/pallas_call | solution.py:279
  274.6 8.1 collective-permute-done.38.refs_6_
  283.8 145.0 %shard_map.486 = bf16[4,8,96,768]{3,2,1,0:T(8,128)(2,1)} custom-call(s32[2]{0:T(128)} %pad_add_fusion.where_ref, bf16[4,96,768]{2,1,0:T(8,128)(2,1)} %pad_maximum_fusion.3.refs_0_, bf16[4,96,768]{2,1,0:T(8,128)(2,1)} %collective-permute-done.21.refs_1_, bf16[4,96,768]{2,1,0:T(8,128)(2,1)} %copy-done.44, bf16[4,96,768]{2,1,0:T(8,128)(2,1)} %collective-permute-done.23.refs_3_, ...), custom_call_target="tpu_custom_call" | custom-call | bytes 10485760 | tf_op jit(solution)/shard_map/pallas_call | solution.py:223
  428.8 19.0 %fusion.9 = (bf16[4,512,768]{2,1,0:T(8,128)(2,1)}, f32[4,512,768]{2,1,0:T(8,128)}, f32[4,768,512]{1,2,0:T(8,128)}) fusion(f32[4,768]{1,0:T(4,128)S(1)} %add.469, bf16[4,768,768]{2,1,0:T(8,128)(2,1)} %bitcast.483, bf16[512,768]{1,0:T(8,128)(2,1)S(1)} %fusion.30), kind=kOutput, calls=%fused_computation.17 | convolution fusion | flops 2519728128 | bytes 21245952 | tf_op jit(solution)/shard_map/td,pdf->ptf/dot_general | solution.py:457
  447.9 145.0 %shard_map.487 = bf16[4,8,96,768]{3,2,1,0:T(8,128)(2,1)} custom-call(s32[2]{0:T(128)} %pad_add_fusion.where_ref, bf16[4,96,768]{2,1,0:T(8,128)(2,1)} %pad_maximum_fusion.4.refs_0_, bf16[4,96,768]{2,1,0:T(8,128)(2,1)} %collective-permute-done.33.refs_1_, bf16[4,96,768]{2,1,0:T(8,128)(2,1)} %collective-permute-done.34.refs_2_, ...), custom_call_target="tpu_custom_call" | custom-call | bytes 10485760 | tf_op jit(solution)/shard_map/pallas_call | solution.py:223
  592.9 6.2 fusion.118
  609.9 7.0 convert_reduce_fusion
  630.2 19.1 %shard_map.489 = (bf16[4,512,576]{2,1,0:T(8,128)(2,1)S(1)}, f32[4,1,576]{2,1,0:T(1,128)S(1)}, f32[512,768]{1,0:T(8,128)S(1)}) custom-call(bf16[512,768]{1,0:T(8,128)(2,1)S(1)} %convert_element_type.321.da_ref, bf16[4,768,768]{2,1,0:T(8,128)(2,1)} %bitcast.480, bf16[4,512,576]{2,1,0:T(8,128)(2,1)S(1)} %copy-done.9, bf16[4,512,192]{2,1,0:T(8,128)(2,1)S(1)} %copy-done.4, ...), custom_call_target="tpu_custom_call" | custom-call | flops 21474836480 | bytes 16777216 | tf_op jit(solution)/shard_map/pallas_call | solution.py:344
  702.8 5.4 collective-permute-done.50
  728.0 9.3 collective-permute-done.61
  743.9 6.0 collective-permute-done.69
  753.4 26.0 %collective-permute-done.60 = bf16[4,96,768]{2,1,0:T(8,128)(2,1)S(1)} collective-permute-done((bf16[4,96,768]{2,1,0:T(8,128)(2,1)S(1)}, bf16[4,96,768]{2,1,0:T(8,128)(2,1)S(1)}, u32[]{:S(2)}, u32[]{:S(2)}) %collective-permute-start.60) | collective-permute-done | bytes 589856 | tf_op jit(solution)/shard_map/ppermute | solution.py:59
  784.5 8.9 collective-permute-done.55
  798.5 8.2 collective-permute-done.73
  810.9 5.0 collective-permute-done.64
  818.6 5.8 stack.283
  826.7 5.8 stack.312
  835.3 96.4 %shard_map.490 = bf16[4,512,768]{2,1,0:T(8,128)(2,1)} custom-call(s32[1]{0:T(128)} %bitcast.rank_ref, bf16[512,768]{1,0:T(8,128)(2,1)} %convert_element_type.322.refs_0_, bf16[512,768]{1,0:T(8,128)(2,1)} %collective-permute-done.45.refs_1_, bf16[512,768]{1,0:T(8,128)(2,1)} %collective-permute-done.46.refs_2_, bf16[512,768]{1,0:T(8,128)(2,1)} %collective-permute-done.47.refs_3_), custom_call_target="tpu_custom_call" | custom-call | bytes 8388608 | tf_op jit(solution)/shard_map/pallas_call | solution.py:176
  932.4 96.4 %shard_map.488 = bf16[4,512,768]{2,1,0:T(8,128)(2,1)} custom-call(s32[1]{0:T(128)} %bitcast.rank_ref, bf16[512,768]{1,0:T(8,128)(2,1)} %get-tuple-element.195.refs_0_, bf16[512,768]{1,0:T(8,128)(2,1)} %collective-permute-done.42.refs_1_, bf16[512,768]{1,0:T(8,128)(2,1)} %collective-permute-done.43.refs_2_, bf16[512,768]{1,0:T(8,128)(2,1)} %collective-permute-done.44.refs_3_), custom_call_target="tpu_custom_call" | custom-call | bytes 8388608 | tf_op jit(solution)/shard_map/pallas_call | solution.py:176
  (528 shorter events, 228.0 us)
Async XLA Ops:
  2.9 30.2 %collective-permute-start.2 = (bf16[96,768]{1,0:T(8,128)(2,1)S(1)}, bf16[96,768]{1,0:T(8,128)(2,1)S(1)}, u32[]{:S(2)}, u32[]{:S(2)}) collective-permute-start(bf16[96,768]{1,0:T(8,128)(2,1)S(1)} %pad_maximum_fusion.6), channel_id=1, source_target_pairs={{0,24},{1,25},{2,26},{3,27},{4,28},{5,29},{6,30},{7,31},{8,16},{9,... | collective-permute-start | bytes 442376 | tf_op jit(solution)/shard_map/ppermute | solution.py:59
  61.5 31.1 %collective-permute-start.36 = (bf16[4,96,768]{2,1,0:T(8,128)(2,1)}, bf16[4,96,768]{2,1,0:T(8,128)(2,1)}, u32[]{:S(2)}, u32[]{:S(2)}) collective-permute-start(bf16[4,96,768]{2,1,0:T(8,128)(2,1)} %pad_maximum_fusion.4.refs_0_), channel_id=1, source_target_pairs={{0,2},{1,3},{2,0},{3,1},{4,6},{5,7},{6,4},{7,5},{8,10},{9,11},{10,... | collective-permute-start | bytes 1769480 | tf_op jit(solution)/shard_map/ppermute | solution.py:59
  70.5 35.9 %collective-permute-start.4 = (bf16[4,96,768]{2,1,0:T(8,128)(2,1)S(1)}, bf16[4,96,768]{2,1,0:T(8,128)(2,1)S(1)}, u32[]{:S(2)}, u32[]{:S(2)}) collective-permute-start(bf16[4,96,768]{2,1,0:T(8,128)(2,1)S(1)} %pad_maximum_fusion.2.refs_0_), channel_id=1, source_target_pairs={{0,1},{1,0},{2,3},{3,2},{4,5},{5,4},{6,7},{7,6},{8,9},{9,8},{10,11... | collective-permute-start | bytes 1769480 | tf_op jit(solution)/shard_map/ppermute | solution.py:59
  106.3 165.8 %collective-permute-start.22 = (bf16[4,96,768]{2,1,0:T(8,128)(2,1)}, bf16[4,96,768]{2,1,0:T(8,128)(2,1)S(1)}, u32[]{:S(2)}, u32[]{:S(2)}) collective-permute-start(bf16[4,96,768]{2,1,0:T(8,128)(2,1)} %pad_maximum_fusion.3.refs_0_), channel_id=1, source_target_pairs={{0,1},{1,0},{2,3},{3,2},{4,5},{5,4},{6,7},{7,6},{8,9},{9,8},{10,11... | collective-permute-start | bytes 1769480 | tf_op jit(solution)/shard_map/ppermute | solution.py:59
  106.4 166.6 %collective-permute-start.25 = (bf16[2,96,768]{2,1,0:T(8,128)(2,1)}, bf16[2,96,768]{2,1,0:T(8,128)(2,1)}, u32[]{:S(2)}, u32[]{:S(2)}) collective-permute-start(bf16[2,96,768]{2,1,0:T(8,128)(2,1)} %slice.419), channel_id=1, source_target_pairs={{0,2},{1,3},{2,0},{3,1},{4,6},{5,7},{6,4},{7,5},{8,10},{9,11},{10,... | collective-permute-start | bytes 884744 | tf_op jit(solution)/shard_map/ppermute | solution.py:59
  107.9 165.8 %collective-permute-start.26 = (bf16[2,96,768]{2,1,0:T(8,128)(2,1)}, bf16[2,96,768]{2,1,0:T(8,128)(2,1)}, u32[]{:S(2)}, u32[]{:S(2)}) collective-permute-start(bf16[2,96,768]{2,1,0:T(8,128)(2,1)} %slice.420), channel_id=1, source_target_pairs={{0,4},{1,5},{2,6},{3,7},{4,0},{5,1},{6,2},{7,3},{8,12},{9,13},{10,... | collective-permute-start | bytes 884744 | tf_op jit(solution)/shard_map/ppermute | solution.py:59
  109.4 164.5 %collective-permute-start.37 = (bf16[2,96,768]{2,1,0:T(8,128)(2,1)}, bf16[2,96,768]{2,1,0:T(8,128)(2,1)S(1)}, u32[]{:S(2)}, u32[]{:S(2)}) collective-permute-start(bf16[2,96,768]{2,1,0:T(8,128)(2,1)} %slice.422), channel_id=1, source_target_pairs={{0,2},{1,3},{2,0},{3,1},{4,6},{5,7},{6,4},{7,5},{8,10},{9,11},{10,... | collective-permute-start | bytes 884744 | tf_op jit(solution)/shard_map/ppermute | solution.py:59
  110.0 172.7 %collective-permute-start.23 = (bf16[4,96,768]{2,1,0:T(8,128)(2,1)}, bf16[4,96,768]{2,1,0:T(8,128)(2,1)}, u32[]{:S(2)}, u32[]{:S(2)}) collective-permute-start(bf16[4,96,768]{2,1,0:T(8,128)(2,1)} %collective-permute-done.21.refs_1_), channel_id=1, source_target_pairs={{0,1},{1,0},{2,3},{3,2},{4,5},{5,4},{6,7},{7,6},{8,9},{9,8},{10,11... | collective-permute-start | bytes 1769480 | tf_op jit(solution)/shard_map/ppermute | solution.py:59
  282.7 165.2 %collective-permute-start.34 = (bf16[4,96,768]{2,1,0:T(8,128)(2,1)}, bf16[4,96,768]{2,1,0:T(8,128)(2,1)}, u32[]{:S(2)}, u32[]{:S(2)}) collective-permute-start(bf16[4,96,768]{2,1,0:T(8,128)(2,1)} %pad_maximum_fusion.4.refs_0_), channel_id=1, source_target_pairs={{0,1},{1,0},{2,3},{3,2},{4,5},{5,4},{6,7},{7,6},{8,9},{9,8},{10,11... | collective-permute-start | bytes 1769480 | tf_op jit(solution)/shard_map/ppermute | solution.py:59
  282.7 165.2 %collective-permute-start.35 = (bf16[4,96,768]{2,1,0:T(8,128)(2,1)}, bf16[4,96,768]{2,1,0:T(8,128)(2,1)}, u32[]{:S(2)}, u32[]{:S(2)}) collective-permute-start(bf16[4,96,768]{2,1,0:T(8,128)(2,1)} %collective-permute-done.33.refs_1_), channel_id=1, source_target_pairs={{0,1},{1,0},{2,3},{3,2},{4,5},{5,4},{6,7},{7,6},{8,9},{9,8},{10,11... | collective-permute-start | bytes 1769480 | tf_op jit(solution)/shard_map/ppermute | solution.py:59
  283.2 164.7 %collective-permute-start.39 = (bf16[4,96,768]{2,1,0:T(8,128)(2,1)}, bf16[4,96,768]{2,1,0:T(8,128)(2,1)}, u32[]{:S(2)}, u32[]{:S(2)}) collective-permute-start(bf16[4,96,768]{2,1,0:T(8,128)(2,1)} %collective-permute-done.36.refs_4_), channel_id=1, source_target_pairs={{0,1},{1,0},{2,3},{3,2},{4,5},{5,4},{6,7},{7,6},{8,9},{9,8},{10,11... | collective-permute-start | bytes 1769480 | tf_op jit(solution)/shard_map/ppermute | solution.py:59
  283.3 164.6 %collective-permute-start.40 = (bf16[2,96,768]{2,1,0:T(8,128)(2,1)S(1)}, bf16[2,96,768]{2,1,0:T(8,128)(2,1)}, u32[]{:S(2)}, u32[]{:S(2)}) collective-permute-start(bf16[2,96,768]{2,1,0:T(8,128)(2,1)S(1)} %collective-permute-done.37.refs_5_), channel_id=1, source_target_pairs={{0,1},{1,0},{2,3},{3,2},{4,5},{5,4},{6,7},{7,6},{8,9},{9,8},{10,11... | collective-permute-start | bytes 884744 | tf_op jit(solution)/shard_map/ppermute | solution.py:59
  283.8 164.2 %collective-permute-start.41 = (bf16[2,96,768]{2,1,0:T(8,128)(2,1)}, bf16[2,96,768]{2,1,0:T(8,128)(2,1)}, u32[]{:S(2)}, u32[]{:S(2)}) collective-permute-start(bf16[2,96,768]{2,1,0:T(8,128)(2,1)} %collective-permute-done.38.refs_6_), channel_id=1, source_target_pairs={{0,1},{1,0},{2,3},{3,2},{4,5},{5,4},{6,7},{7,6},{8,9},{9,8},{10,11... | collective-permute-start | bytes 884744 | tf_op jit(solution)/shard_map/ppermute | solution.py:59
  669.2 45.3 %collective-permute-start.66 = (bf16[768,768]{1,0:T(8,128)(2,1)}, bf16[768,768]{1,0:T(8,128)(2,1)}, u32[]{:S(2)}, u32[]{:S(2)}) collective-permute-start(bf16[768,768]{1,0:T(8,128)(2,1)} %convolution_convert_fusion.2), channel_id=1, source_target_pairs={{0,1},{1,0},{2,3},{3,2},{4,5},{5,4},{6,7},{7,6},{8,9},{9,8},{10,11... | collective-permute-start | bytes 3538952 | tf_op jit(solution)/shard_map/ppermute | solution.py:59
  689.1 36.5 %collective-permute-start.57 = (bf16[768,768]{1,0:T(8,128)(2,1)}, bf16[768,768]{1,0:T(8,128)(2,1)}, u32[]{:S(2)}, u32[]{:S(2)}) collective-permute-start(bf16[768,768]{1,0:T(8,128)(2,1)} %convolution_convert_fusion.6), channel_id=1, source_target_pairs={{0,1},{1,0},{2,3},{3,2},{4,5},{5,4},{6,7},{7,6},{8,9},{9,8},{10,11... | collective-permute-start | bytes 3538952 | tf_op jit(solution)/shard_map/ppermute | solution.py:59
  737.3 72.9 %collective-permute-start.46 = (bf16[512,768]{1,0:T(8,128)(2,1)S(1)}, bf16[512,768]{1,0:T(8,128)(2,1)}, u32[]{:S(2)}, u32[]{:S(2)}) collective-permute-start(bf16[512,768]{1,0:T(8,128)(2,1)S(1)} %copy-done.18), channel_id=1, source_target_pairs={{0,2},{1,3},{2,0},{3,1},{4,6},{5,7},{6,4},{7,5},{8,10},{9,11},{10,... | collective-permute-start | bytes 2359304 | tf_op jit(solution)/shard_map/ppermute | solution.py:59
  739.9 39.5 %collective-permute-start.60 = (bf16[4,96,768]{2,1,0:T(8,128)(2,1)S(1)}, bf16[4,96,768]{2,1,0:T(8,128)(2,1)S(1)}, u32[]{:S(2)}, u32[]{:S(2)}) collective-permute-start(bf16[4,96,768]{2,1,0:T(8,128)(2,1)S(1)} %fusion.36), channel_id=1, source_target_pairs={{0,2},{1,3},{2,0},{3,1},{4,6},{5,7},{6,4},{7,5},{8,10},{9,11},{10,... | collective-permute-start | bytes 1769480 | tf_op jit(solution)/shard_map/ppermute | solution.py:59
  740.7 39.7 %collective-permute-start.62 = (bf16[4,96,768]{2,1,0:T(8,128)(2,1)S(1)}, bf16[4,96,768]{2,1,0:T(8,128)(2,1)S(1)}, u32[]{:S(2)}, u32[]{:S(2)}) collective-permute-start(bf16[4,96,768]{2,1,0:T(8,128)(2,1)S(1)} %fusion.35), channel_id=1, source_target_pairs={{0,4},{1,5},{2,6},{3,7},{4,0},{5,1},{6,2},{7,3},{8,12},{9,13},{10,... | collective-permute-start | bytes 1769480 | tf_op jit(solution)/shard_map/ppermute | solution.py:59
  749.9 60.4 %collective-permute-start.43 = (bf16[512,768]{1,0:T(8,128)(2,1)S(1)}, bf16[512,768]{1,0:T(8,128)(2,1)}, u32[]{:S(2)}, u32[]{:S(2)}) collective-permute-start(bf16[512,768]{1,0:T(8,128)(2,1)S(1)} %copy-done.19), channel_id=1, source_target_pairs={{0,2},{1,3},{2,0},{3,1},{4,6},{5,7},{6,4},{7,5},{8,10},{9,11},{10,... | collective-permute-start | bytes 2359304 | tf_op jit(solution)/shard_map/ppermute | solution.py:59
  751.2 32.7 %collective-permute-start.54 = (bf16[96,768]{1,0:T(8,128)(2,1)S(1)}, bf16[96,768]{1,0:T(8,128)(2,1)S(1)}, u32[]{:S(2)}, u32[]{:S(2)}) collective-permute-start(bf16[96,768]{1,0:T(8,128)(2,1)S(1)} %get-tuple-element.206), channel_id=1, source_target_pairs={{0,8},{1,9},{2,10},{3,11},{4,12},{5,13},{6,14},{7,15},{8,0},{9,1},... | collective-permute-start | bytes 442376 | tf_op jit(solution)/shard_map/ppermute | solution.py:59
  810.3 122.1 %collective-permute-start.42 = (bf16[512,768]{1,0:T(8,128)(2,1)S(1)}, bf16[512,768]{1,0:T(8,128)(2,1)}, u32[]{:S(2)}, u32[]{:S(2)}) collective-permute-start(bf16[512,768]{1,0:T(8,128)(2,1)S(1)} %copy-done.19), channel_id=1, source_target_pairs={{0,1},{1,0},{2,3},{3,2},{4,5},{5,4},{6,7},{7,6},{8,9},{9,8},{10,11... | collective-permute-start | bytes 2359304 | tf_op jit(solution)/shard_map/ppermute | solution.py:59
  815.9 116.6 %collective-permute-start.44 = (bf16[512,768]{1,0:T(8,128)(2,1)}, bf16[512,768]{1,0:T(8,128)(2,1)}, u32[]{:S(2)}, u32[]{:S(2)}) collective-permute-start(bf16[512,768]{1,0:T(8,128)(2,1)} %collective-permute-done.43.refs_2_), channel_id=1, source_target_pairs={{0,1},{1,0},{2,3},{3,2},{4,5},{5,4},{6,7},{7,6},{8,9},{9,8},{10,11... | collective-permute-start | bytes 2359304 | tf_op jit(solution)/shard_map/ppermute | solution.py:59
  833.9 97.8 %collective-permute-start.82 = (f32[2,15]{1,0:T(2,128)S(1)}, f32[2,15]{1,0:T(2,128)S(1)}, u32[]{:S(2)}, u32[]{:S(2)}) collective-permute-start(f32[2,15]{1,0:T(2,128)S(1)} %fusion.97), channel_id=1, source_target_pairs={{0,2},{1,3},{2,0},{3,1},{4,6},{5,7},{6,4},{7,5},{8,10},{9,11},{10,... | collective-permute-start | bytes 368 | tf_op jit(solution)/shard_map/ppermute | solution.py:59
  931.8 97.2 %collective-permute-start.83 = (f32[2,15]{1,0:T(2,128)S(1)}, f32[2,15]{1,0:T(2,128)S(1)}, u32[]{:S(2)}, u32[]{:S(2)}) collective-permute-start(f32[2,15]{1,0:T(2,128)S(1)} %fusion.139), channel_id=1, source_target_pairs={{0,4},{1,5},{2,6},{3,7},{4,0},{5,1},{6,2},{7,3},{8,12},{9,13},{10,... | collective-permute-start | bytes 368 | tf_op jit(solution)/shard_map/ppermute | solution.py:59
  (146 other events, 1954.8 us)
